TPU v7x, 32 devices: a whole 2x2x4 slice. The times are simulated.
32 devices in a mesh: groups: 2 (over y), rowf: 4 (over z), colf: 4 (over x, core).
Axes of the slice: x: 2, y: 2, z: 4, core: 2. Of those that a mesh axis runs over, the one named last changes fastest.
Arguments:
- embeddings: bfloat16 [1024, 256, 64], P(('groups', 'rowf'), 'colf'), parts along dimension 0, may hold values from -6 to 6
- pair_weights: bfloat16 [256, 128, 64, 64], P('colf', 'rowf'), may hold values from -0.09375 to 0.09375
- upstream: bfloat16 [1024, 256, 128], P('groups', 'colf', 'rowf'), parts along dimension 0, may hold values from -1.5 to 1.5
Outputs:
- interact: bfloat16 [1024, 256, 128], P('groups', 'colf', 'rowf'), parts along dimension 0
- grad_pair: bfloat16 [512, 128, 64, 64], P(('groups', 'colf'), 'rowf'), parts along dimension 0
- grad_emb: float32 [1024, 256, 64], P(('groups', 'rowf'), 'colf'), parts along dimension 0
There are 2 independent parts, one for each index of `groups`. A program takes and returns all parts, laid end to end along the dimension named above; an argument that names none is the same for every part. Nothing has to cross between parts.
All inputs are finite; a program needn't handle non-finite values.
Results may differ from a plain program's by a relative error of at most 0.0049.
Values may be sent and summed in bfloat16 or wider, within the bound.
A program may use at most 320 MiB of HBM per device.

v0:
```python
import jax
import jax.numpy as jnp
from jax import lax
from jax.sharding import PartitionSpec as P


def passed_along(shard, axis, by):
    count = lax.axis_size(axis)
    return lax.ppermute(shard, axis, [(i, (i + by) % count) for i in range(count)])


def slide_back(block, steps):
    return passed_along(block.astype(jnp.bfloat16), "colf", steps).astype(block.dtype)


def fetch_from(block, distance):
    return passed_along(block, "colf", -distance)


def shards(embeddings, pair_weights, upstream):
    n_rowf = lax.axis_size("rowf")
    row_id = lax.axis_index("rowf")
    col_id = lax.axis_index("colf")
    a_dev = pair_weights.shape[0]
    off_dev = pair_weights.shape[1]
    emb_width = pair_weights.shape[2]
    half_fields = off_dev * n_rowf
    block_ratio = a_dev // off_dev
    lead_blocks = row_id // block_ratio
    shift_in = row_id % block_ratio * off_dev
    lead_top = (n_rowf - 1) // block_ratio
    n_bits = lead_top.bit_length()
    count_groups = a_dev // 4
    own_block = lax.all_gather(embeddings, "rowf", axis=0, tiled=True)
    batch_rows = own_block.shape[0]
    pieces = [own_block]
    for distance in range(1, lead_top + 2):
        pieces.append(fetch_from(own_block, distance))
    shifted = pieces[0]
    following = pieces[1]
    for distance in range(1, lead_top + 1):
        shifted = jnp.where(lead_blocks == distance, pieces[distance], shifted)
        following = jnp.where(lead_blocks == distance, pieces[distance + 1], following)
    window = jnp.concatenate([shifted, following], axis=1)
    first_ids = col_id * a_dev + jnp.arange(a_dev, dtype=jnp.int32)
    offset_ids = row_id * off_dev + jnp.arange(off_dev, dtype=jnp.int32)
    dead = jnp.logical_and(
        offset_ids[None, :] == half_fields - 1, first_ids[:, None] >= half_fields
    )
    pair_mask = 1.0 - dead.astype(jnp.float32)

    def compute(col_win, group_idx):
        row_start = group_idx * 4
        emb_group = lax.dynamic_slice_in_dim(own_block, row_start, 4, 1)
        weight_group = lax.dynamic_slice_in_dim(pair_weights, row_start, 4, 0)
        up_group = lax.dynamic_slice_in_dim(upstream, row_start, 4, 1).astype(jnp.float32)
        mask_group = lax.dynamic_slice_in_dim(pair_mask, row_start, 4, 0)
        starts = [row_start + member + 1 + shift_in for member in range(4)]
        partner = jnp.stack(
            [lax.dynamic_slice_in_dim(window, start_at, off_dev, 1) for start_at in starts], axis=1
        ).astype(jnp.float32)
        projected = jnp.einsum(
            "bik,ijkl->bijl", emb_group, weight_group, preferred_element_type=jnp.float32
        )
        interact = (jnp.sum(projected * partner, axis=3) * mask_group).astype(jnp.bfloat16)
        scaled = up_group * mask_group
        weighted = (scaled[..., None] * partner).astype(jnp.bfloat16)
        grad_pair = jnp.einsum(
            "bik,bijl->ijkl", emb_group, weighted, preferred_element_type=jnp.float32
        ).astype(jnp.bfloat16)
        row_terms = jnp.einsum(
            "bijl,ijkl->bik", weighted, weight_group, preferred_element_type=jnp.float32
        )
        col_piece = scaled[..., None] * projected
        for member in range(4):
            current = lax.dynamic_slice_in_dim(col_win, starts[member], off_dev, 1)
            col_win = lax.dynamic_update_slice_in_dim(
                col_win, current + col_piece[:, member], starts[member], 1
            )
        return (col_win, (interact, grad_pair, row_terms))

    start_win = jnp.zeros((batch_rows, 2 * a_dev, emb_width), jnp.float32)
    col_win, (interact, grad_pair, row_terms) = lax.scan(
        compute, start_win, jnp.arange(count_groups, dtype=jnp.int32)
    )
    interact = jnp.transpose(interact, (1, 0, 2, 3)).reshape(batch_rows, a_dev, off_dev)
    grad_pair = grad_pair.reshape(a_dev, off_dev, emb_width, emb_width)
    row_terms = jnp.transpose(row_terms, (1, 0, 2, 3)).reshape(batch_rows, a_dev, emb_width)
    lower_part = col_win[:, :a_dev]
    upper_part = col_win[:, a_dev:]
    carried = lower_part + slide_back(upper_part, 1)
    for bit_pos in range(n_bits):
        fetched = slide_back(carried, 1 << bit_pos)
        carried = jnp.where(lead_blocks >> bit_pos & 1 == 1, fetched, carried)
    grad_emb = lax.psum_scatter(row_terms + carried, "rowf", scatter_dimension=0, tiled=True)
    return (interact, grad_pair, grad_emb)


def solution(mesh):
    return jax.shard_map(
        shards,
        mesh=mesh,
        in_specs=(
            P(("groups", "rowf"), "colf", None),
            P("colf", "rowf", None, None),
            P("groups", "colf", "rowf"),
        ),
        out_specs=(
            P("groups", "colf", "rowf"),
            P(("groups", "colf"), "rowf", None, None),
            P(("groups", "rowf"), "colf", None),
        ),
        check_vma=False,
    )
```

profile of v0, /device:TPU:0, one launch (start us, length us, event | category | flops | bytes accessed | tf_op | source)
XLA Modules:
  0.0 1421.1 jit_solution(16117428509840055184)
XLA Ops:
  7.9 84.9 %all-gather.2.cloned.1.call-done = bf16[512,64,64]{0,2,1:T(8,128)(2,1)} async-done(((bf16[128,64,64]{0,2,1:T(8,128)(2,1)}), bf16[512,64,64]{0,2,1:T(8,128)(2,1)}) %all-gather.2.cloned.1.call-update) | async-done | bytes 4194320 | tf_op jit(solution)/shard_map/all_gather | solution.py:34
  94.4 91.2 %collective-permute-done.1 = bf16[512,64,64]{0,2,1:T(8,128)(2,1)} collective-permute-done((bf16[512,64,64]{0,2,1:T(8,128)(2,1)}, bf16[512,64,64]{0,2,1:T(8,128)(2,1)}, u32[]{:S(2)}, u32[]{:S(2)}) %collective-permute-start.1) | collective-permute-done | bytes 4194336 | tf_op jit(solution)/shard_map/ppermute | solution.py:9
  185.6 44.0 %collective-permute-done = bf16[512,64,64]{0,2,1:T(8,128)(2,1)} collective-permute-done((bf16[512,64,64]{0,2,1:T(8,128)(2,1)}, bf16[512,64,64]{0,2,1:T(8,128)(2,1)}, u32[]{:S(2)}, u32[]{:S(2)}) %collective-permute-start) | collective-permute-done | bytes 4194336 | tf_op jit(solution)/shard_map/ppermute | solution.py:9
  229.6 5.8 broadcast_select_fusion.1
  235.4 7.4 pad_maximum_fusion.3
  242.8 7.9 broadcast_in_dim.34
  250.7 899.3 %while.18 = (s32[]{:T(128)}, f32[512,128,64]{0,2,1:T(8,128)}, bf16[16,512,4,32]{1,3,2,0:T(8,128)(2,1)}, bf16[16,4,32,64,64]{4,3,2,1,0:T(8,128)(2,1)}, f32[16,512...) while((s32[]{:T(128)}, f32[512,128,64]{0,2,1:T(8,128)}, ...), condition=%wide.region_2.3_spmd, body=%wide.region_0.2_spmd.sunk | while | flops 1695219712 | bytes 281808640 | solution.py:83
  268.7 6.7 fusion.60
  275.4 10.3 fusion.54
  324.9 6.7 fusion.60
  331.5 10.3 fusion.54
  381.1 6.7 fusion.60
  387.7 10.3 fusion.54
  437.2 6.7 fusion.60
  443.9 10.4 fusion.54
  493.4 6.7 fusion.60
  500.1 10.3 fusion.54
  549.6 6.7 fusion.60
  556.3 10.4 fusion.54
  605.8 6.7 fusion.60
  612.5 10.4 fusion.54
  646.2 4.8 dynamic-slice_bitcast_fusion.5
  662.2 6.7 fusion.60
  668.9 10.3 fusion.54
  702.5 4.7 dynamic-slice_bitcast_fusion.5
  718.4 6.7 fusion.60
  725.1 10.4 fusion.54
  774.7 6.7 fusion.60
  781.4 10.4 fusion.54
  815.1 4.8 dynamic-slice_bitcast_fusion.5
  831.1 6.7 fusion.60
  837.8 10.3 fusion.54
  871.4 4.8 dynamic-slice_bitcast_fusion.5
  887.4 6.7 fusion.60
  894.1 10.3 fusion.54
  943.6 6.7 fusion.60
  950.3 10.3 fusion.54
  999.7 6.7 fusion.60
  1006.4 10.3 fusion.54
  1055.8 6.7 fusion.60
  1062.5 10.3 fusion.54
  1111.9 6.7 fusion.60
  1118.6 10.3 fusion.54
  1155.1 47.3 %collective-permute-done.2 = bf16[512,64,64]{0,2,1:T(8,128)(2,1)S(1)} collective-permute-done((bf16[512,64,64]{0,2,1:T(8,128)(2,1)S(1)}, bf16[512,64,64]{0,2,1:T(8,128)(2,1)S(1)}, u32[]{:S(2)}, u32[]{:S(2)}) %collective-permute-start.2) | collective-permute-done | bytes 4194336 | tf_op jit(solution)/shard_map/ppermute | solution.py:9
  1202.4 8.4 fusion.38
  1210.8 48.2 %collective-permute-done.3 = bf16[512,64,64]{0,2,1:T(8,128)(2,1)} collective-permute-done((bf16[512,64,64]{0,2,1:T(8,128)(2,1)}, bf16[512,64,64]{0,2,1:T(8,128)(2,1)}, u32[]{:S(2)}, u32[]{:S(2)}) %collective-permute-start.3) | collective-permute-done | bytes 4194336 | tf_op jit(solution)/shard_map/ppermute | solution.py:9
  1259.0 13.4 bitcast_add_fusion
  1272.4 141.9 %reduce-scatter.2.cloned.1.call-done = f32[128,64,64]{0,2,1:T(8,128)} async-done(((f32[512,64,64]{0,2,1:T(8,128)}), f32[128,64,64]{0,2,1:T(8,128)}) %reduce-scatter.2.cloned.1.call-update) | async-done | bytes 2097168 | tf_op jit(solution)/shard_map/reduce_scatter | solution.py:95
  (542 shorter events, 602.1 us)
Async XLA Ops:
  7.2 85.7 %all-gather.2.cloned.1.call-start = ((), (), s32[]{:S(2)}) async-start(), calls=%async_computation.1 | async-start | bytes 5242880 | tf_op jit(solution)/shard_map/all_gather | solution.py:34
  7.9 1406.4 %reduce-scatter.2.cloned.1.call-start = ((), (), s32[]{:S(2)}) async-start(), calls=%async_computation.2 | async-start | bytes 10485760 | tf_op jit(solution)/shard_map/reduce_scatter | solution.py:95
  92.9 92.8 %collective-permute-start.1 = (bf16[512,64,64]{0,2,1:T(8,128)(2,1)}, bf16[512,64,64]{0,2,1:T(8,128)(2,1)}, u32[]{:S(2)}, u32[]{:S(2)}) collective-permute-start(bf16[512,64,64]{0,2,1:T(8,128)(2,1)} %all-gather.2.cloned.1.call-done), channel_id=1, source_target_pairs={{0,2},{1,3},{2,0},{3,1},{4,6},{5,7},{6,4},{7,5},{8,10},{9,11},{10,... | collective-permute-start | bytes 12582920 | tf_op jit(solution)/shard_map/ppermute | solution.py:9
  94.3 135.3 %collective-permute-start = (bf16[512,64,64]{0,2,1:T(8,128)(2,1)}, bf16[512,64,64]{0,2,1:T(8,128)(2,1)}, u32[]{:S(2)}, u32[]{:S(2)}) collective-permute-start(bf16[512,64,64]{0,2,1:T(8,128)(2,1)} %all-gather.2.cloned.1.call-done), channel_id=1, source_target_pairs={{0,3},{1,0},{2,1},{3,2},{4,7},{5,4},{6,5},{7,6},{8,11},{9,8},{10,9... | collective-permute-start | bytes 12582920 | tf_op jit(solution)/shard_map/ppermute | solution.py:9
  268.7 17.8 %slice-start = ((s8[16777216]{0:T(1024)(128)(4,1)}), s8[4194304]{0:T(1024)(128)(4,1)S(1)}, s32[]{:S(2)}) async-start(s8[16777216]{0:T(1024)(128)(4,1)} %bitcast.96), calls=%async_computation.3 | async-start | bytes 8388608 | tf_op jit(solution)/shard_map/while
  268.7 17.8 %slice-start.1 = ((s8[16777216]{0:T(1024)(128)(4,1)}), s8[4194304]{0:T(1024)(128)(4,1)S(1)}, s32[]{:S(2)}) async-start(s8[16777216]{0:T(1024)(128)(4,1)} %bitcast.96), calls=%async_computation.4 | async-start | bytes 8388608 | tf_op jit(solution)/shard_map/while
  268.7 17.8 %slice-start.2 = ((s8[16777216]{0:T(1024)(128)(4,1)}), s8[4194304]{0:T(1024)(128)(4,1)S(1)}, s32[]{:S(2)}) async-start(s8[16777216]{0:T(1024)(128)(4,1)} %bitcast.96), calls=%async_computation.5 | async-start | bytes 8388608 | tf_op jit(solution)/shard_map/while
  324.8 17.8 %slice-start = ((s8[16777216]{0:T(1024)(128)(4,1)}), s8[4194304]{0:T(1024)(128)(4,1)S(1)}, s32[]{:S(2)}) async-start(s8[16777216]{0:T(1024)(128)(4,1)} %bitcast.96), calls=%async_computation.3 | async-start | bytes 8388608 | tf_op jit(solution)/shard_map/while
  324.8 17.8 %slice-start.1 = ((s8[16777216]{0:T(1024)(128)(4,1)}), s8[4194304]{0:T(1024)(128)(4,1)S(1)}, s32[]{:S(2)}) async-start(s8[16777216]{0:T(1024)(128)(4,1)} %bitcast.96), calls=%async_computation.4 | async-start | bytes 8388608 | tf_op jit(solution)/shard_map/while
  324.8 17.8 %slice-start.2 = ((s8[16777216]{0:T(1024)(128)(4,1)}), s8[4194304]{0:T(1024)(128)(4,1)S(1)}, s32[]{:S(2)}) async-start(s8[16777216]{0:T(1024)(128)(4,1)} %bitcast.96), calls=%async_computation.5 | async-start | bytes 8388608 | tf_op jit(solution)/shard_map/while
  381.0 17.8 %slice-start = ((s8[16777216]{0:T(1024)(128)(4,1)}), s8[4194304]{0:T(1024)(128)(4,1)S(1)}, s32[]{:S(2)}) async-start(s8[16777216]{0:T(1024)(128)(4,1)} %bitcast.96), calls=%async_computation.3 | async-start | bytes 8388608 | tf_op jit(solution)/shard_map/while
  381.0 17.8 %slice-start.1 = ((s8[16777216]{0:T(1024)(128)(4,1)}), s8[4194304]{0:T(1024)(128)(4,1)S(1)}, s32[]{:S(2)}) async-start(s8[16777216]{0:T(1024)(128)(4,1)} %bitcast.96), calls=%async_computation.4 | async-start | bytes 8388608 | tf_op jit(solution)/shard_map/while
  437.2 17.8 %slice-start = ((s8[16777216]{0:T(1024)(128)(4,1)}), s8[4194304]{0:T(1024)(128)(4,1)S(1)}, s32[]{:S(2)}) async-start(s8[16777216]{0:T(1024)(128)(4,1)} %bitcast.96), calls=%async_computation.3 | async-start | bytes 8388608 | tf_op jit(solution)/shard_map/while
  437.2 17.8 %slice-start.1 = ((s8[16777216]{0:T(1024)(128)(4,1)}), s8[4194304]{0:T(1024)(128)(4,1)S(1)}, s32[]{:S(2)}) async-start(s8[16777216]{0:T(1024)(128)(4,1)} %bitcast.96), calls=%async_computation.4 | async-start | bytes 8388608 | tf_op jit(solution)/shard_map/while
  437.2 17.8 %slice-start.2 = ((s8[16777216]{0:T(1024)(128)(4,1)}), s8[4194304]{0:T(1024)(128)(4,1)S(1)}, s32[]{:S(2)}) async-start(s8[16777216]{0:T(1024)(128)(4,1)} %bitcast.96), calls=%async_computation.5 | async-start | bytes 8388608 | tf_op jit(solution)/shard_map/while
  493.3 17.8 %slice-start = ((s8[16777216]{0:T(1024)(128)(4,1)}), s8[4194304]{0:T(1024)(128)(4,1)S(1)}, s32[]{:S(2)}) async-start(s8[16777216]{0:T(1024)(128)(4,1)} %bitcast.96), calls=%async_computation.3 | async-start | bytes 8388608 | tf_op jit(solution)/shard_map/while
  493.4 17.8 %slice-start.1 = ((s8[16777216]{0:T(1024)(128)(4,1)}), s8[4194304]{0:T(1024)(128)(4,1)S(1)}, s32[]{:S(2)}) async-start(s8[16777216]{0:T(1024)(128)(4,1)} %bitcast.96), calls=%async_computation.4 | async-start | bytes 8388608 | tf_op jit(solution)/shard_map/while
  549.6 17.8 %slice-start = ((s8[16777216]{0:T(1024)(128)(4,1)}), s8[4194304]{0:T(1024)(128)(4,1)S(1)}, s32[]{:S(2)}) async-start(s8[16777216]{0:T(1024)(128)(4,1)} %bitcast.96), calls=%async_computation.3 | async-start | bytes 8388608 | tf_op jit(solution)/shard_map/while
  549.6 17.8 %slice-start.1 = ((s8[16777216]{0:T(1024)(128)(4,1)}), s8[4194304]{0:T(1024)(128)(4,1)S(1)}, s32[]{:S(2)}) async-start(s8[16777216]{0:T(1024)(128)(4,1)} %bitcast.96), calls=%async_computation.4 | async-start | bytes 8388608 | tf_op jit(solution)/shard_map/while
  549.6 17.8 %slice-start.2 = ((s8[16777216]{0:T(1024)(128)(4,1)}), s8[4194304]{0:T(1024)(128)(4,1)S(1)}, s32[]{:S(2)}) async-start(s8[16777216]{0:T(1024)(128)(4,1)} %bitcast.96), calls=%async_computation.5 | async-start | bytes 8388608 | tf_op jit(solution)/shard_map/while
  605.8 17.8 %slice-start = ((s8[16777216]{0:T(1024)(128)(4,1)}), s8[4194304]{0:T(1024)(128)(4,1)S(1)}, s32[]{:S(2)}) async-start(s8[16777216]{0:T(1024)(128)(4,1)} %bitcast.96), calls=%async_computation.3 | async-start | bytes 8388608 | tf_op jit(solution)/shard_map/while
  605.8 17.8 %slice-start.1 = ((s8[16777216]{0:T(1024)(128)(4,1)}), s8[4194304]{0:T(1024)(128)(4,1)S(1)}, s32[]{:S(2)}) async-start(s8[16777216]{0:T(1024)(128)(4,1)} %bitcast.96), calls=%async_computation.4 | async-start | bytes 8388608 | tf_op jit(solution)/shard_map/while
  605.8 17.8 %slice-start.2 = ((s8[16777216]{0:T(1024)(128)(4,1)}), s8[4194304]{0:T(1024)(128)(4,1)S(1)}, s32[]{:S(2)}) async-start(s8[16777216]{0:T(1024)(128)(4,1)} %bitcast.96), calls=%async_computation.5 | async-start | bytes 8388608 | tf_op jit(solution)/shard_map/while
  662.1 17.8 %slice-start = ((s8[16777216]{0:T(1024)(128)(4,1)}), s8[4194304]{0:T(1024)(128)(4,1)S(1)}, s32[]{:S(2)}) async-start(s8[16777216]{0:T(1024)(128)(4,1)} %bitcast.96), calls=%async_computation.3 | async-start | bytes 8388608 | tf_op jit(solution)/shard_map/while
  662.1 17.8 %slice-start.1 = ((s8[16777216]{0:T(1024)(128)(4,1)}), s8[4194304]{0:T(1024)(128)(4,1)S(1)}, s32[]{:S(2)}) async-start(s8[16777216]{0:T(1024)(128)(4,1)} %bitcast.96), calls=%async_computation.4 | async-start | bytes 8388608 | tf_op jit(solution)/shard_map/while
  662.2 17.8 %slice-start.2 = ((s8[16777216]{0:T(1024)(128)(4,1)}), s8[4194304]{0:T(1024)(128)(4,1)S(1)}, s32[]{:S(2)}) async-start(s8[16777216]{0:T(1024)(128)(4,1)} %bitcast.96), calls=%async_computation.5 | async-start | bytes 8388608 | tf_op jit(solution)/shard_map/while
  718.4 17.8 %slice-start = ((s8[16777216]{0:T(1024)(128)(4,1)}), s8[4194304]{0:T(1024)(128)(4,1)S(1)}, s32[]{:S(2)}) async-start(s8[16777216]{0:T(1024)(128)(4,1)} %bitcast.96), calls=%async_computation.3 | async-start | bytes 8388608 | tf_op jit(solution)/shard_map/while
  718.4 17.8 %slice-start.1 = ((s8[16777216]{0:T(1024)(128)(4,1)}), s8[4194304]{0:T(1024)(128)(4,1)S(1)}, s32[]{:S(2)}) async-start(s8[16777216]{0:T(1024)(128)(4,1)} %bitcast.96), calls=%async_computation.4 | async-start | bytes 8388608 | tf_op jit(solution)/shard_map/while
  718.4 17.8 %slice-start.2 = ((s8[16777216]{0:T(1024)(128)(4,1)}), s8[4194304]{0:T(1024)(128)(4,1)S(1)}, s32[]{:S(2)}) async-start(s8[16777216]{0:T(1024)(128)(4,1)} %bitcast.96), calls=%async_computation.5 | async-start | bytes 8388608 | tf_op jit(solution)/shard_map/while
  774.7 17.8 %slice-start = ((s8[16777216]{0:T(1024)(128)(4,1)}), s8[4194304]{0:T(1024)(128)(4,1)S(1)}, s32[]{:S(2)}) async-start(s8[16777216]{0:T(1024)(128)(4,1)} %bitcast.96), calls=%async_computation.3 | async-start | bytes 8388608 | tf_op jit(solution)/shard_map/while
  774.7 17.8 %slice-start.1 = ((s8[16777216]{0:T(1024)(128)(4,1)}), s8[4194304]{0:T(1024)(128)(4,1)S(1)}, s32[]{:S(2)}) async-start(s8[16777216]{0:T(1024)(128)(4,1)} %bitcast.96), calls=%async_computation.4 | async-start | bytes 8388608 | tf_op jit(solution)/shard_map/while
  774.7 17.8 %slice-start.2 = ((s8[16777216]{0:T(1024)(128)(4,1)}), s8[4194304]{0:T(1024)(128)(4,1)S(1)}, s32[]{:S(2)}) async-start(s8[16777216]{0:T(1024)(128)(4,1)} %bitcast.96), calls=%async_computation.5 | async-start | bytes 8388608 | tf_op jit(solution)/shard_map/while
  831.1 17.8 %slice-start = ((s8[16777216]{0:T(1024)(128)(4,1)}), s8[4194304]{0:T(1024)(128)(4,1)S(1)}, s32[]{:S(2)}) async-start(s8[16777216]{0:T(1024)(128)(4,1)} %bitcast.96), calls=%async_computation.3 | async-start | bytes 8388608 | tf_op jit(solution)/shard_map/while
  887.4 17.8 %slice-start = ((s8[16777216]{0:T(1024)(128)(4,1)}), s8[4194304]{0:T(1024)(128)(4,1)S(1)}, s32[]{:S(2)}) async-start(s8[16777216]{0:T(1024)(128)(4,1)} %bitcast.96), calls=%async_computation.3 | async-start | bytes 8388608 | tf_op jit(solution)/shard_map/while
  887.4 17.8 %slice-start.1 = ((s8[16777216]{0:T(1024)(128)(4,1)}), s8[4194304]{0:T(1024)(128)(4,1)S(1)}, s32[]{:S(2)}) async-start(s8[16777216]{0:T(1024)(128)(4,1)} %bitcast.96), calls=%async_computation.4 | async-start | bytes 8388608 | tf_op jit(solution)/shard_map/while
  943.6 17.8 %slice-start = ((s8[16777216]{0:T(1024)(128)(4,1)}), s8[4194304]{0:T(1024)(128)(4,1)S(1)}, s32[]{:S(2)}) async-start(s8[16777216]{0:T(1024)(128)(4,1)} %bitcast.96), calls=%async_computation.3 | async-start | bytes 8388608 | tf_op jit(solution)/shard_map/while
  943.6 17.8 %slice-start.1 = ((s8[16777216]{0:T(1024)(128)(4,1)}), s8[4194304]{0:T(1024)(128)(4,1)S(1)}, s32[]{:S(2)}) async-start(s8[16777216]{0:T(1024)(128)(4,1)} %bitcast.96), calls=%async_computation.4 | async-start | bytes 8388608 | tf_op jit(solution)/shard_map/while
  943.6 17.8 %slice-start.2 = ((s8[16777216]{0:T(1024)(128)(4,1)}), s8[4194304]{0:T(1024)(128)(4,1)S(1)}, s32[]{:S(2)}) async-start(s8[16777216]{0:T(1024)(128)(4,1)} %bitcast.96), calls=%async_computation.5 | async-start | bytes 8388608 | tf_op jit(solution)/shard_map/while
  999.7 17.8 %slice-start = ((s8[16777216]{0:T(1024)(128)(4,1)}), s8[4194304]{0:T(1024)(128)(4,1)S(1)}, s32[]{:S(2)}) async-start(s8[16777216]{0:T(1024)(128)(4,1)} %bitcast.96), calls=%async_computation.3 | async-start | bytes 8388608 | tf_op jit(solution)/shard_map/while
  999.7 17.8 %slice-start.1 = ((s8[16777216]{0:T(1024)(128)(4,1)}), s8[4194304]{0:T(1024)(128)(4,1)S(1)}, s32[]{:S(2)}) async-start(s8[16777216]{0:T(1024)(128)(4,1)} %bitcast.96), calls=%async_computation.4 | async-start | bytes 8388608 | tf_op jit(solution)/shard_map/while
  1055.7 17.8 %slice-start = ((s8[16777216]{0:T(1024)(128)(4,1)}), s8[4194304]{0:T(1024)(128)(4,1)S(1)}, s32[]{:S(2)}) async-start(s8[16777216]{0:T(1024)(128)(4,1)} %bitcast.96), calls=%async_computation.3 | async-start | bytes 8388608 | tf_op jit(solution)/shard_map/while
  1055.8 17.8 %slice-start.1 = ((s8[16777216]{0:T(1024)(128)(4,1)}), s8[4194304]{0:T(1024)(128)(4,1)S(1)}, s32[]{:S(2)}) async-start(s8[16777216]{0:T(1024)(128)(4,1)} %bitcast.96), calls=%async_computation.4 | async-start | bytes 8388608 | tf_op jit(solution)/shard_map/while
  1055.8 17.8 %slice-start.2 = ((s8[16777216]{0:T(1024)(128)(4,1)}), s8[4194304]{0:T(1024)(128)(4,1)S(1)}, s32[]{:S(2)}) async-start(s8[16777216]{0:T(1024)(128)(4,1)} %bitcast.96), calls=%async_computation.5 | async-start | bytes 8388608 | tf_op jit(solution)/shard_map/while
  1111.9 17.8 %slice-start = ((s8[16777216]{0:T(1024)(128)(4,1)}), s8[4194304]{0:T(1024)(128)(4,1)S(1)}, s32[]{:S(2)}) async-start(s8[16777216]{0:T(1024)(128)(4,1)} %bitcast.96), calls=%async_computation.3 | async-start | bytes 8388608 | tf_op jit(solution)/shard_map/while
  1111.9 17.8 %slice-start.1 = ((s8[16777216]{0:T(1024)(128)(4,1)}), s8[4194304]{0:T(1024)(128)(4,1)S(1)}, s32[]{:S(2)}) async-start(s8[16777216]{0:T(1024)(128)(4,1)} %bitcast.96), calls=%async_computation.4 | async-start | bytes 8388608 | tf_op jit(solution)/shard_map/while
  1111.9 17.8 %slice-start.2 = ((s8[16777216]{0:T(1024)(128)(4,1)}), s8[4194304]{0:T(1024)(128)(4,1)S(1)}, s32[]{:S(2)}) async-start(s8[16777216]{0:T(1024)(128)(4,1)} %bitcast.96), calls=%async_computation.5 | async-start | bytes 8388608 | tf_op jit(solution)/shard_map/while
  1154.0 48.4 %collective-permute-start.2 = (bf16[512,64,64]{0,2,1:T(8,128)(2,1)S(1)}, bf16[512,64,64]{0,2,1:T(8,128)(2,1)S(1)}, u32[]{:S(2)}, u32[]{:S(2)}) collective-permute-start(bf16[512,64,64]{0,2,1:T(8,128)(2,1)S(1)} %slice.64), channel_id=1, source_target_pairs={{0,1},{1,2},{2,3},{3,0},{4,5},{5,6},{6,7},{7,4},{8,9},{9,10},{10,1... | collective-permute-start | bytes 12582920 | tf_op jit(solution)/shard_map/ppermute | solution.py:9
  1210.8 48.2 %collective-permute-start.3 = (bf16[512,64,64]{0,2,1:T(8,128)(2,1)}, bf16[512,64,64]{0,2,1:T(8,128)(2,1)}, u32[]{:S(2)}, u32[]{:S(2)}) collective-permute-start(bf16[512,64,64]{0,2,1:T(8,128)(2,1)} %fusion.38), channel_id=1, source_target_pairs={{0,1},{1,2},{2,3},{3,0},{4,5},{5,6},{6,7},{7,4},{8,9},{9,10},{10,1... | collective-permute-start | bytes 12582920 | tf_op jit(solution)/shard_map/ppermute | solution.py:9
  (119 other events, 651.2 us)
Sparse Core Ops, SparseCore 0:
  9.6 83.2 all-gather.1
  1272.5 141.7 reduce-scatter.1
where the time goes:
time: 1430 us; the launch traced here: 1420 us
  waiting for transfers between devices  458 us (32%)
  matrix products  347 us (24%)
  local copies, waits for them, and re-layouts  300 us (21%)
  other arithmetic  285 us (20%)
    ppermute x4, waiting for transfers between devices, passed_along(): lax.ppermute(shard, axis, [(i, (i + by) % count) for i in range(count)])  231 us
    dynamic_update_slice x64, other arithmetic, compute(): lax.dynamic_update_slice_in_dim(col_win, current + col_piece[:, member],...  223 us
    dot_general x16, matrix products, compute(): jnp.einsum('bik,ijkl->bijl', emb_group, weight_group, preferred_element_t...  165 us
    reduce_scatter x1, waiting for transfers between devices, shards(): lax.psum_scatter(row_terms + carried, 'rowf', scatter_dimension=0, tiled=...  142 us
    while x320, local copies, waits for them, and re-layouts  129 us
    dot_general x16, matrix products, compute(): jnp.einsum('bijl,ijkl->bik', weighted, weight_group, preferred_element_ty...  107 us
    all_gather x1, waiting for transfers between devices, shards(): own_block = lax.all_gather(embeddings, 'rowf', axis=0, tiled=True)  84.9 us
    dynamic_update_slice x32, local copies, waits for them, and re-layouts, shards(): lax.scan(compute, start_win, jnp.arange(count_groups, dtype=jnp.int32))  75.3 us
  transfers between devices with their start and end apart: 6, of which 6 were waited for; matrix products, arithmetic and copies ran while one was open for 0% of the time, Pallas kernels for 0%

commit v1 on v0

v1 whole, which is shorter than its diff:
```python
import functools

import jax
import jax.numpy as jnp
from jax import lax
from jax.experimental import pallas as pl
from jax.experimental.pallas import tpu as pltpu
from jax.sharding import PartitionSpec as P

F32 = jnp.float32
BF16 = jnp.bfloat16
MEMBERS = 4


def pair_kernel(dead_ref, own_ref, up_ref, weight_ref, near_ref, far_ref, *rest, with_start):
    if with_start:
        start_ref, _, _, *rest = rest
    (interact_ref, grad_ref, row_ref, col_near_ref, col_far_ref, window, col, sems) = rest
    step = pl.program_id(0)
    n_off = weight_ref.shape[1]
    width, batch = own_ref.shape[1:]

    @pl.when(step == 0)
    def _():
        copies = [
            pltpu.make_async_copy(near_ref, window.at[pl.ds(0, n_off)], sems.at[0]),
            pltpu.make_async_copy(far_ref, window.at[pl.ds(n_off, n_off)], sems.at[1]),
        ]
        if with_start:
            copies.append(pltpu.make_async_copy(start_ref, col.at[pl.ds(0, n_off)], sems.at[2]))
        else:
            col[0:n_off] = jnp.zeros((n_off, width, batch), F32)
        for copy in copies:
            copy.start()
        col[n_off:] = jnp.zeros((n_off, width, batch), F32)
        for copy in copies:
            copy.wait()

    own = own_ref[0]
    rows = lax.broadcasted_iota(jnp.int32, (n_off, batch), 0)
    dead = jnp.logical_and(rows == n_off - 1, step >= dead_ref[0])
    scaled = jnp.where(dead, 0.0, up_ref[0].astype(F32))
    total = jnp.zeros((width, batch), F32)
    dots = []
    for first in range(0, n_off, MEMBERS):
        members = range(first, first + MEMBERS)
        mats = [weight_ref[0, d] for d in members]
        weighted = jnp.concatenate(
            [window[step + d + 1] * scaled[d : d + 1].astype(BF16) for d in members], axis=0
        )
        turned = jnp.concatenate([mat.T for mat in mats], axis=0)
        projected = jnp.dot(turned, own, preferred_element_type=F32)
        for at, d in enumerate(members):
            piece = projected[at * width : (at + 1) * width]
            partner = window[step + d + 1].astype(F32)
            dots.append(jnp.sum(piece * partner, axis=0, keepdims=True))
            col[step + d + 1] += scaled[d : d + 1] * piece
        total = total + jnp.dot(
            jnp.concatenate(mats, axis=1), weighted, preferred_element_type=F32
        )
        grads = lax.dot_general(
            weighted, own, (((1,), (1,)), ((), ())), preferred_element_type=F32
        )
        for at, d in enumerate(members):
            grad_ref[0, d] = grads[at * width : (at + 1) * width].T.astype(BF16)
    interact = jnp.where(dead, 0.0, jnp.concatenate(dots, axis=0))
    interact_ref[0] = interact.astype(BF16)
    row_ref[0] = total

    @pl.when(step == pl.num_programs(0) - 1)
    def _():
        col_near_ref[...] = col[0:n_off].astype(col_near_ref.dtype)
        col_far_ref[...] = col[n_off:].astype(col_far_ref.dtype)


def pair_block(part, dead_from, own, up, weights, near, far, earlier, far_type):
    n_off, width = weights.shape[1], weights.shape[2]
    batch = own.shape[2]
    block = (n_off, width, batch)
    anywhere = pl.BlockSpec(memory_space=pl.ANY)
    pairs = n_off * n_off
    in_specs = [
        pl.BlockSpec(memory_space=pltpu.SMEM),
        pl.BlockSpec((1, width, batch), lambda i: (i, 0, 0)),
        pl.BlockSpec((1, n_off, batch), lambda i: (part * n_off + i, 0, 0)),
        pl.BlockSpec((1, n_off, width, width), lambda i: (part * n_off + i, 0, 0, 0)),
        anywhere,
        anywhere,
    ]
    args = [dead_from, own, up, weights, near, far]
    aliases = {}
    if earlier:
        aliases = {len(args) + 1: 0, len(args) + 2: 1}
        in_specs += [anywhere] * 3
        args += earlier
    whole = pl.BlockSpec(block, lambda i: (0, 0, 0), pipeline_mode=pl.Buffered(1))
    return pl.pallas_call(
        functools.partial(pair_kernel, with_start=len(earlier) > 0),
        grid=(n_off,),
        in_specs=in_specs,
        out_specs=[
            pl.BlockSpec((1, n_off, batch), lambda i: (part * n_off + i, 0, 0)),
            pl.BlockSpec((1, n_off, width, width), lambda i: (part * n_off + i, 0, 0, 0)),
            pl.BlockSpec((1, width, batch), lambda i: (i, 0, 0)),
            whole,
            whole,
        ],
        out_shape=[
            jax.ShapeDtypeStruct(up.shape, BF16),
            jax.ShapeDtypeStruct(weights.shape, BF16),
            jax.ShapeDtypeStruct(block, F32),
            jax.ShapeDtypeStruct(block, BF16),
            jax.ShapeDtypeStruct(block, far_type),
        ],
        scratch_shapes=[
            pltpu.VMEM((2 * n_off, width, batch), BF16),
            pltpu.VMEM((2 * n_off, width, batch), F32),
            pltpu.SemaphoreType.DMA((3,)),
        ],
        input_output_aliases=aliases,
        compiler_params=pltpu.CompilerParams(vmem_limit_bytes=52 * 2**20),
        cost_estimate=pl.CostEstimate(
            flops=24 * pairs * batch * width * width,
            bytes_accessed=8 * pairs * width * width,
            transcendentals=0,
        ),
    )(*args)


def choose(options, index):
    out = options[0]
    for at in range(1, len(options)):
        out = jnp.where(index == at, options[at], out)
    return out


def shards(embeddings, pair_weights, upstream):
    n_rowf, n_colf = lax.axis_size("rowf"), lax.axis_size("colf")
    row_id, col_id = lax.axis_index("rowf"), lax.axis_index("colf")
    a_dev, off_dev = pair_weights.shape[0], pair_weights.shape[1]
    half_fields = off_dev * n_rowf
    parts = a_dev // off_dev
    emb = jnp.transpose(embeddings, (1, 2, 0))
    up = jnp.transpose(upstream, (1, 2, 0))

    def moved(block, distance, back=False):
        pairs = []
        for r in range(n_rowf):
            for c in range(n_colf):
                ahead = r * n_colf + (c + distance(r)) % n_colf
                here = r * n_colf + c
                pairs.append((here, ahead) if back else (ahead, here))
        return lax.ppermute(block, ("rowf", "colf"), pairs)

    own = [
        lax.all_gather(emb[m * off_dev : (m + 1) * off_dev], "rowf", axis=2, tiled=True)
        for m in range(parts)
    ]
    fetched = [
        moved(own[m], lambda r, m=m: (r + (m - r) % parts) // parts) for m in range(parts)
    ]
    windows = [choose(fetched, (row_id + w) % parts) for w in range(parts)]
    windows.append(moved(choose(own, row_id % parts), lambda r: (r + parts) // parts))

    row_parts, returned, earlier = [], [], []
    for part in range(parts):
        last = part == parts - 1
        dead_from = half_fields - col_id * a_dev - part * off_dev
        dead_from = jnp.where(row_id == n_rowf - 1, dead_from, off_dev).astype(jnp.int32)
        interact, grad, row, near, far = pair_block(
            part, dead_from.reshape(1), own[part], up, pair_weights,
            windows[part], windows[part + 1], earlier, BF16 if last else F32,
        )
        row_parts.append(row)
        returned.append(moved(near, lambda r, w=part: (r + w) // parts, True))
        earlier = [far, interact, grad]
    returned.append(moved(far, lambda r: (r + parts) // parts, True))
    terms = [item.astype(F32) for item in returned]
    terms = [terms[0] + terms[parts]] + terms[1:parts]
    outs = []
    for m in range(parts):
        carried = choose(terms, (m - row_id) % parts)
        summed = (row_parts[m] + carried).astype(BF16)
        outs.append(lax.psum_scatter(summed, "rowf", scatter_dimension=2, tiled=True))
    grad_emb = jnp.concatenate(outs, axis=0).astype(F32)
    return (
        jnp.transpose(interact, (2, 0, 1)),
        grad,
        jnp.transpose(grad_emb, (2, 0, 1)),
    )


def solution(mesh):
    return jax.shard_map(
        shards,
        mesh=mesh,
        in_specs=(
            P(("groups", "rowf"), "colf", None),
            P("colf", "rowf", None, None),
            P("groups", "colf", "rowf"),
        ),
        out_specs=(
            P("groups", "colf", "rowf"),
            P(("groups", "colf"), "rowf", None, None),
            P(("groups", "rowf"), "colf", None),
        ),
        check_vma=False,
    )
```

time: 1430 us -> 519 us (0.36)
  matrix products: 347 us -> 0 us
  other arithmetic: 285 us -> 15.6 us
  local copies, waits for them, and re-layouts: 300 us -> 37.5 us
  waiting for transfers between devices: 458 us -> 291 us
  Pallas kernels: 0 us -> 117 us
  starting transfers between devices: 2.59 us -> 40.3 us
    dot_general x48 -> x0, matrix products: 347 us -> none  [the longest x16 165 us: compute(): jnp.einsum('bik,ijkl->bijl', emb_group, weight_group, preferred_element_t...]
    dynamic_update_slice x80 -> x0, other arithmetic: 235 us -> none  [the longest x64 223 us: compute(): lax.dynamic_update_slice_in_dim(col_win, current + col_piece[:, member],...]
    ppermute x4 -> x6, waiting for transfers between devices: 231 us -> 8.68 us  [moved(): return lax.ppermute(block, ('rowf', 'colf'), pairs)]
    unnamed x2 -> x6, waiting for transfers between devices: 0.7 us -> 189 us
    reduce_scatter x1 -> x0, waiting for transfers between devices: 142 us -> none  [shards(): lax.psum_scatter(row_terms + carried, 'rowf', scatter_dimension=0, tiled=...]
    while x320 -> x0, local copies, waits for them, and re-layouts: 129 us -> none
    pallas_call x0 -> x2, Pallas kernels: none -> 117 us  [pair_block(): pl.pallas_call(functools.partial(pair_kernel, with_start=len(earlier) > 0...]
    dynamic_update_slice x32 -> x0, local copies, waits for them, and re-layouts: 75.3 us -> none  [shards(): lax.scan(compute, start_win, jnp.arange(count_groups, dtype=jnp.int32))]
  transfers between devices with their start and end apart: 6 -> 10, of which waited for: 6 -> 5; matrix products, arithmetic and copies ran while one was open for 0% -> 4% of each run, Pallas kernels for 0% -> 11%
where the time goes in v1:
time: 519 us; the launch traced here: 516 us
  waiting for transfers between devices  291 us (56%)
  Pallas kernels  117 us (23%)
  starting transfers between devices  40.3 us (8%)
  local copies, waits for them, and re-layouts  37.5 us (7%)
  other arithmetic  15.6 us (3%)
  between operations  13.8 us (3%)
    unnamed x6, waiting for transfers between devices  189 us
    pallas_call x2, Pallas kernels, pair_block(): pl.pallas_call(functools.partial(pair_kernel, with_start=len(earlier) > 0...  117 us
    all_gather x2, waiting for transfers between devices, shards(): lax.all_gather(emb[m * off_dev:(m + 1) * off_dev], 'rowf', axis=2, tiled=...  93.2 us
    ppermute x6, starting transfers between devices, moved(): return lax.ppermute(block, ('rowf', 'colf'), pairs)  39.9 us
    unnamed x12, local copies, waits for them, and re-layouts  35.2 us
  transfers between devices with their start and end apart: 10, of which 5 were waited for; matrix products, arithmetic and copies ran while one was open for 4% of the time, Pallas kernels for 11%

profile of v1, /device:TPU:0, one launch (start us, length us, event | category | flops | bytes accessed | tf_op | source)
XLA Modules:
  0.0 515.7 jit_solution(3621541774312829611)
XLA Ops:
  7.2 0.0 all-gather.3.cloned.1.call-start
  7.2 2.2 fusion.4
  9.4 0.0 all-gather.3.cloned.1.call-update
  9.5 0.0 all-gather.5.cloned.1.call-start
  9.5 0.7 all-gather.5.cloned.1.call-update
  10.2 0.0 reduce-scatter.9.cloned.1.call-start
  10.3 48.8 %all-gather.3.cloned.1.call-done.own_ref = bf16[32,64,512]{2,1,0:T(8,128)(2,1)} async-done(((bf16[32,64,128]{2,1,0:T(8,128)(2,1)}), bf16[32,64,512]{2,1,0:T(8,128)(2,1)}) %all-gather.3.cloned.1.call-update) | async-done | bytes 2097168 | tf_op jit(solution)/shard_map/all_gather | solution.py:156
  59.1 2.2 collective-permute-start
  61.3 44.4 %all-gather.5.cloned.1.call-done.own_ref = bf16[32,64,512]{2,1,0:T(8,128)(2,1)} async-done(((bf16[32,64,128]{2,1,0:T(8,128)(2,1)}), bf16[32,64,512]{2,1,0:T(8,128)(2,1)}) %all-gather.5.cloned.1.call-update) | async-done | bytes 2097168 | tf_op jit(solution)/shard_map/all_gather | solution.py:156
  105.7 17.1 %collective-permute-start.1 = (bf16[32,64,512]{2,1,0:T(8,128)(2,1)}, bf16[32,64,512]{2,1,0:T(8,128)(2,1)}, u32[]{:S(2)}, u32[]{:S(2)}) collective-permute-start(bf16[32,64,512]{2,1,0:T(8,128)(2,1)} %all-gather.5.cloned.1.call-done.own_ref), channel_id=1, source_target_pairs={{0,0},{1,1},{2,2},{3,3},{5,4},{6,5},{7,6},{4,7},{9,8},{10,9},{11,1... | collective-permute-start | bytes 6291464 | tf_op jit(solution)/shard_map/ppermute | solution.py:153
  122.8 1.8 broadcast_select_fusion.1
  124.7 1.2 collective-permute-start.2
  125.9 0.0 collective-permute-done
  125.9 0.0 collective-permute-done.1
  125.9 3.9 broadcast_select_fusion
  129.8 58.2 %shard_map.58 = (bf16[64,32,512]{2,1,0:T(8,128)(2,1)}, bf16[64,32,64,64]{3,2,1,0:T(8,128)(2,1)}, f32[32,64,512]{2,1,0:T(8,128)}, bf16[32,64,512]{2,1,0:T(8,128)(2,1)}, f32[32,64,512]{2,1,0:T(8,128)}) custom-call(s32[1]{0:T(128)} %bitcast.7.dead_ref, bf16[32,64,512]{2,1,0:T(8,128)(2,1)} %all-gather.5.cloned.1.call-done.own_ref, ...), custom_call_target="tpu_custom_call" | custom-call | flops 51539607552 | bytes 33554432 | tf_op jit(solution)/shard_map/pallas_call | solution.py:97
  188.0 0.0 collective-permute-done.2.far_ref
  188.0 0.0 copy-start.1
  188.0 1.3 copy-done.1
  189.3 59.0 %shard_map.59 = (bf16[64,32,512]{2,1,0:T(8,128)(2,1)}, bf16[64,32,64,64]{3,2,1,0:T(8,128)(2,1)}, f32[32,64,512]{2,1,0:T(8,128)}, bf16[32,64,512]{2,1,0:T(8,128)(2,1)}, bf16[32,64,512]{2,1,0:T(8,128)(2,1)}) custom-call(s32[1]{0:T(128)} %bitcast.4.dead_ref, ...), custom_call_target="tpu_custom_call", output_to_operand_aliasing={{0}: (7, {}), {1}: (8, {})} | custom-call | flops 51539607552 | bytes 33554432 | tf_op jit(solution)/shard_map/pallas_call | solution.py:97
  248.3 2.2 collective-permute-start.3
  250.5 0.0 collective-permute-start.5
  250.6 17.1 %collective-permute-start.4 = (bf16[32,64,512]{2,1,0:T(8,128)(2,1)}, bf16[32,64,512]{2,1,0:T(8,128)(2,1)}, u32[]{:S(2)}, u32[]{:S(2)}) collective-permute-start(bf16[32,64,512]{2,1,0:T(8,128)(2,1)} %get-tuple-element.20), channel_id=1, source_target_pairs={{0,0},{1,1},{2,2},{3,3},{4,4},{5,5},{6,6},{7,7},{8,9},{9,10},{10,1... | collective-permute-start | bytes 6291464 | tf_op jit(solution)/shard_map/ppermute | solution.py:153
  267.7 0.0 collective-permute-done.3
  267.7 0.0 copy-start
  267.7 8.7 %collective-permute-done.5 = bf16[32,64,512]{2,1,0:T(8,128)(2,1)} collective-permute-done((bf16[32,64,512]{2,1,0:T(8,128)(2,1)}, bf16[32,64,512]{2,1,0:T(8,128)(2,1)}, u32[]{:S(2)}, u32[]{:S(2)}) %collective-permute-start.5) | collective-permute-done | bytes 2097184 | tf_op jit(solution)/shard_map/ppermute | solution.py:153
  276.3 0.0 collective-permute-done.4
  276.3 0.0 copy-done
  276.3 8.4 %fusion.1 = (bf16[32,64,512]{2,1,0:T(8,128)(2,1)S(1)}, bf16[32,64,512]{2,1,0:T(8,128)(2,1)}) fusion(f32[32,64,512]{2,1,0:T(8,128)} %get-tuple-element.18, bf16[32,64,512]{2,1,0:T(8,128)(2,1)} %copy-done, bf16[32,64,512]{2,1,0:T(8,128)(2,1)} %collective-permute-done.5, bf16[32,64,512]{2,1,0:T(8,128)(2,1)} %collective-permute-done.4, pred[]{:T(512)S(6)} %eq.26, ...), kind=kLoop, calls=%fused_computation.3 | loop fusion | flops 10485760 | bytes 18874370 | tf_op jit(solution)/shard_map/convert_element_type | solution.py:183
  284.7 7.4 %copy.10 = bf16[32,64,512]{1,0,2:T(8,128)(2,1)} copy(bf16[32,64,512]{2,1,0:T(8,128)(2,1)} %get-tuple-element.24) | data formatting | bytes 4194304
  292.2 6.7 %reshape.16 = bf16[512,2048]{1,0:T(8,128)(2,1)} reshape(bf16[512,32,64]{2,1,0:T(8,128)(2,1)} %bitcast.11) | data formatting | bytes 4194304
  298.9 0.0 reduce-scatter.9.cloned.1.call-update
  298.9 0.2 reduce-scatter.7.cloned.1.call-start
  299.2 6.6 %copy.8 = bf16[32,64,512]{1,0,2:T(8,128)(2,1)} copy(bf16[32,64,512]{2,1,0:T(8,128)(2,1)S(1)} %get-tuple-element.23) | data formatting | bytes 4194304
  305.8 6.8 %reshape.14 = bf16[512,2048]{1,0:T(8,128)(2,1)} reshape(bf16[512,32,64]{2,1,0:T(8,128)(2,1)} %bitcast.12) | data formatting | bytes 4194304
  312.6 0.0 reduce-scatter.7.cloned.1.call-update
  312.6 146.4 %reduce-scatter.9.cloned.1.call-done = bf16[128,2048]{1,0:T(8,128)(2,1)} async-done(((bf16[512,2048]{1,0:T(8,128)(2,1)}), bf16[128,2048]{1,0:T(8,128)(2,1)}) %reduce-scatter.9.cloned.1.call-update) | async-done | bytes 524304
  459.0 2.1 reshape.17
  461.1 1.1 copy.11
  462.2 42.3 %reduce-scatter.7.cloned.1.call-done = bf16[128,2048]{1,0:T(8,128)(2,1)} async-done(((bf16[512,2048]{1,0:T(8,128)(2,1)}), bf16[128,2048]{1,0:T(8,128)(2,1)}) %reduce-scatter.7.cloned.1.call-update) | async-done | bytes 524304
  504.5 2.1 reshape.15
  506.6 1.1 copy.9
  507.7 1.5 convert_bitcast_fusion
Async XLA Ops:
  7.2 51.9 %all-gather.3.cloned.1.call-start = ((), (), s32[]{:S(2)}) async-start(), calls=%async_computation.2 | async-start | bytes 2621440 | tf_op jit(solution)/shard_map/all_gather | solution.py:156
  9.5 96.3 %all-gather.5.cloned.1.call-start = ((), (), s32[]{:S(2)}) async-start(), calls=%async_computation.3 | async-start | bytes 2621440 | tf_op jit(solution)/shard_map/all_gather | solution.py:156
  10.2 448.8 %reduce-scatter.9.cloned.1.call-start = ((), (), s32[]{:S(2)}) async-start(), calls=%async_computation.5 | async-start | bytes 2621440
  59.1 66.8 %collective-permute-start = (bf16[32,64,512]{2,1,0:T(8,128)(2,1)}, bf16[32,64,512]{2,1,0:T(8,128)(2,1)S(1)}, u32[]{:S(2)}, u32[]{:S(2)}) collective-permute-start(bf16[32,64,512]{2,1,0:T(8,128)(2,1)} %all-gather.3.cloned.1.call-done.own_ref), channel_id=1, source_target_pairs={{0,0},{1,1},{2,2},{3,3},{4,4},{5,5},{6,6},{7,7},{9,8},{10,9},{11,1... | collective-permute-start | bytes 6291464 | tf_op jit(solution)/shard_map/ppermute | solution.py:153
  105.7 20.2 %collective-permute-start.1 = (bf16[32,64,512]{2,1,0:T(8,128)(2,1)}, bf16[32,64,512]{2,1,0:T(8,128)(2,1)}, u32[]{:S(2)}, u32[]{:S(2)}) collective-permute-start(bf16[32,64,512]{2,1,0:T(8,128)(2,1)} %all-gather.5.cloned.1.call-done.own_ref), channel_id=1, source_target_pairs={{0,0},{1,1},{2,2},{3,3},{5,4},{6,5},{7,6},{4,7},{9,8},{10,9},{11,1... | collective-permute-start | bytes 6291464 | tf_op jit(solution)/shard_map/ppermute | solution.py:153
  124.7 63.3 %collective-permute-start.2 = (bf16[32,64,512]{2,1,0:T(8,128)(2,1)S(1)}, bf16[32,64,512]{2,1,0:T(8,128)(2,1)S(1)}, u32[]{:S(2)}, u32[]{:S(2)}) collective-permute-start(bf16[32,64,512]{2,1,0:T(8,128)(2,1)S(1)} %broadcast_select_fusion.1), channel_id=1, source_target_pairs={{1,0},{2,1},{3,2},{0,3},{5,4},{6,5},{7,6},{4,7},{10,8},{11,9},{8,1... | collective-permute-start | bytes 6291464 | tf_op jit(solution)/shard_map/ppermute | solution.py:153
  188.0 1.3 copy-start.1
  248.3 19.4 %collective-permute-start.3 = (bf16[32,64,512]{2,1,0:T(8,128)(2,1)}, bf16[32,64,512]{2,1,0:T(8,128)(2,1)S(1)}, u32[]{:S(2)}, u32[]{:S(2)}) collective-permute-start(bf16[32,64,512]{2,1,0:T(8,128)(2,1)} %get-tuple-element.19), channel_id=1, source_target_pairs={{0,0},{1,1},{2,2},{3,3},{4,5},{5,6},{6,7},{7,4},{8,9},{9,10},{10,1... | collective-permute-start | bytes 6291464 | tf_op jit(solution)/shard_map/ppermute | solution.py:153
  250.5 25.8 %collective-permute-start.5 = (bf16[32,64,512]{2,1,0:T(8,128)(2,1)}, bf16[32,64,512]{2,1,0:T(8,128)(2,1)}, u32[]{:S(2)}, u32[]{:S(2)}) collective-permute-start(bf16[32,64,512]{2,1,0:T(8,128)(2,1)} %get-tuple-element.21), channel_id=1, source_target_pairs={{0,1},{1,2},{2,3},{3,0},{4,5},{5,6},{6,7},{7,4},{8,10},{9,11},{10,... | collective-permute-start | bytes 6291464 | tf_op jit(solution)/shard_map/ppermute | solution.py:153
  250.6 25.8 %collective-permute-start.4 = (bf16[32,64,512]{2,1,0:T(8,128)(2,1)}, bf16[32,64,512]{2,1,0:T(8,128)(2,1)}, u32[]{:S(2)}, u32[]{:S(2)}) collective-permute-start(bf16[32,64,512]{2,1,0:T(8,128)(2,1)} %get-tuple-element.20), channel_id=1, source_target_pairs={{0,0},{1,1},{2,2},{3,3},{4,4},{5,5},{6,6},{7,7},{8,9},{9,10},{10,1... | collective-permute-start | bytes 6291464 | tf_op jit(solution)/shard_map/ppermute | solution.py:153
  267.7 8.7 %copy-start = (bf16[32,64,512]{2,1,0:T(8,128)(2,1)}, bf16[32,64,512]{2,1,0:T(8,128)(2,1)S(1)}, u32[]{:S(2)}) copy-start(bf16[32,64,512]{2,1,0:T(8,128)(2,1)S(1)} %collective-permute-done.3) | copy-start | bytes 6291460
  298.9 205.6 %reduce-scatter.7.cloned.1.call-start = ((), (), s32[]{:S(2)}) async-start(), calls=%async_computation.4 | async-start | bytes 2621440
Sparse Core Ops, SparseCore 0:
  10.1 48.9 all-gather.2
  61.2 44.4 all-gather.4
  299.1 159.9 reduce-scatter.8
  461.3 43.1 reduce-scatter.6

commit v2 on v1

--- a/solution.py
+++ b/solution.py
@@ -160,9 +160,11 @@
         moved(own[m], lambda r, m=m: (r + (m - r) % parts) // parts) for m in range(parts)
     ]
     windows = [choose(fetched, (row_id + w) % parts) for w in range(parts)]
-    windows.append(moved(choose(own, row_id % parts), lambda r: (r + parts) // parts))
-
-    row_parts, returned, earlier = [], [], []
+    held = choose(own, row_id % parts)
+    held, windows[parts - 1] = lax.optimization_barrier((held, windows[parts - 1]))
+    windows.append(moved(held, lambda r: (r + parts) // parts))
+
+    row_parts, cols, earlier = [], [], []
     for part in range(parts):
         last = part == parts - 1
         dead_from = half_fields - col_id * a_dev - part * off_dev
@@ -172,16 +174,27 @@
             windows[part], windows[part + 1], earlier, BF16 if last else F32,
         )
         row_parts.append(row)
-        returned.append(moved(near, lambda r, w=part: (r + w) // parts, True))
+        cols.append(near)
         earlier = [far, interact, grad]
-    returned.append(moved(far, lambda r: (r + parts) // parts, True))
-    terms = [item.astype(F32) for item in returned]
-    terms = [terms[0] + terms[parts]] + terms[1:parts]
+    cols.append(far)
+    first_back = moved(cols[0], lambda r: r // parts, True)
     outs = []
+    shape = (off_dev, emb.shape[1], n_rowf, emb.shape[2])
+    backs = []
     for m in range(parts):
-        carried = choose(terms, (m - row_id) % parts)
-        summed = (row_parts[m] + carried).astype(BF16)
-        outs.append(lax.psum_scatter(summed, "rowf", scatter_dimension=2, tiled=True))
+        sent = choose(cols[1:], (m - row_id - 1) % parts)
+        if m == 0:
+            sent, first_back = lax.optimization_barrier((sent, first_back))
+        else:
+            sent, backs[-1] = lax.optimization_barrier((sent, backs[-1]))
+        backs.append(moved(sent, lambda r, m=m: (r + (m - r - 1) % parts + 1) // parts, True))
+    for m in range(parts):
+        if m > 0:
+            backs[m], summed = lax.optimization_barrier((backs[m], summed))
+        summed = row_parts[m] + backs[m].astype(F32)
+        summed = summed + jnp.where(row_id % parts == m, first_back.astype(F32), 0.0)
+        summed = jnp.transpose(summed.astype(BF16).reshape(shape), (2, 0, 1, 3))
+        outs.append(lax.psum_scatter(summed, "rowf", scatter_dimension=0, tiled=False))
     grad_emb = jnp.concatenate(outs, axis=0).astype(F32)
     return (
         jnp.transpose(interact, (2, 0, 1)),

time: 519 us -> 446 us (0.86)
  local copies, waits for them, and re-layouts: 37.5 us -> 3.55 us
  waiting for transfers between devices: 291 us -> 262 us
  starting transfers between devices: 40.3 us -> 25.2 us
  other arithmetic: 15.6 us -> 22.3 us
    unnamed x6 -> x4, waiting for transfers between devices: 189 us -> 0.74 us
    reduce_scatter x0 -> x2, waiting for transfers between devices: none -> 142 us  [shards(): lax.psum_scatter(summed, 'rowf', scatter_dimension=0, tiled=False)]
    unnamed x12 -> x2, local copies, waits for them, and re-layouts: 35.2 us -> 1.32 us
    ppermute x6, waiting for transfers between devices: 8.68 us -> 25.8 us  [moved(): return lax.ppermute(block, ('rowf', 'colf'), pairs)]
    ppermute x6, starting transfers between devices: 39.9 us -> 25.1 us  [moved(): return lax.ppermute(block, ('rowf', 'colf'), pairs)]
    transpose x0 -> x2, other arithmetic: none -> 9.43 us  [shards(): summed = jnp.transpose(summed.astype(BF16).reshape(shape), (2, 0, 1, 3))]
    convert_element_type x1 -> x0, other arithmetic: 8.41 us -> none  [shards(): summed = (row_parts[m] + carried).astype(BF16)]
  transfers between devices with their start and end apart: 10 -> 10, of which waited for: 5 -> 5; matrix products, arithmetic and copies ran while one was open for 4% -> 2% of each run, Pallas kernels for 11% -> 26%
where the time goes in v2:
time: 446 us; the launch traced here: 444 us
  waiting for transfers between devices  262 us (59%)
  Pallas kernels  117 us (26%)
  starting transfers between devices  25.2 us (6%)
  other arithmetic  22.3 us (5%)
  between operations  13.8 us (3%)
    reduce_scatter x2, waiting for transfers between devices, shards(): lax.psum_scatter(summed, 'rowf', scatter_dimension=0, tiled=False)  142 us
    pallas_call x2, Pallas kernels, pair_block(): pl.pallas_call(functools.partial(pair_kernel, with_start=len(earlier) > 0...  117 us
    all_gather x2, waiting for transfers between devices, shards(): lax.all_gather(emb[m * off_dev:(m + 1) * off_dev], 'rowf', axis=2, tiled=...  93.2 us
    ppermute x6, waiting for transfers between devices, moved(): return lax.ppermute(block, ('rowf', 'colf'), pairs)  25.8 us
    ppermute x6, starting transfers between devices, moved(): return lax.ppermute(block, ('rowf', 'colf'), pairs)  25.1 us
    select_n x3, other arithmetic, choose(): out = jnp.where(index == at, options[at], out)  10.2 us
    transpose x2, other arithmetic, shards(): summed = jnp.transpose(summed.astype(BF16).reshape(shape), (2, 0, 1, 3))  9.43 us
  transfers between devices with their start and end apart: 10, of which 5 were waited for; matrix products, arithmetic and copies ran while one was open for 2% of the time, Pallas kernels for 26%

profile of v2, /device:TPU:0, one launch (start us, length us, event | category | flops | bytes accessed | tf_op | source)
XLA Modules:
  0.0 444.0 jit_solution(10901100945642027385)
XLA Ops:
  7.2 0.0 all-gather.3.cloned.1.call-start
  7.2 2.2 fusion.6
  9.4 0.0 all-gather.3.cloned.1.call-update
  9.5 0.0 all-gather.5.cloned.1.call-start
  9.5 0.7 all-gather.5.cloned.1.call-update
  10.2 0.0 reduce-scatter.3.cloned.1.call-start
  10.3 48.8 %all-gather.3.cloned.1.call-done.own_ref = bf16[32,64,512]{2,1,0:T(8,128)(2,1)} async-done(((bf16[32,64,128]{2,1,0:T(8,128)(2,1)}), bf16[32,64,512]{2,1,0:T(8,128)(2,1)}) %all-gather.3.cloned.1.call-update) | async-done | bytes 2097168 | tf_op jit(solution)/shard_map/all_gather | solution.py:156
  59.1 2.2 collective-permute-start
  61.3 44.4 %all-gather.5.cloned.1.call-done.own_ref = bf16[32,64,512]{2,1,0:T(8,128)(2,1)} async-done(((bf16[32,64,128]{2,1,0:T(8,128)(2,1)}), bf16[32,64,512]{2,1,0:T(8,128)(2,1)}) %all-gather.5.cloned.1.call-update) | async-done | bytes 2097168 | tf_op jit(solution)/shard_map/all_gather | solution.py:156
  105.7 17.2 %collective-permute-start.1 = (bf16[32,64,512]{2,1,0:T(8,128)(2,1)}, bf16[32,64,512]{2,1,0:T(8,128)(2,1)}, u32[]{:S(2)}, u32[]{:S(2)}) collective-permute-start(bf16[32,64,512]{2,1,0:T(8,128)(2,1)} %all-gather.5.cloned.1.call-done.own_ref), channel_id=1, source_target_pairs={{0,0},{1,1},{2,2},{3,3},{5,4},{6,5},{7,6},{4,7},{9,8},{10,9},{11,1... | collective-permute-start | bytes 6291464 | tf_op jit(solution)/shard_map/ppermute | solution.py:153
  122.9 1.8 broadcast_select_fusion.4
  124.7 0.0 collective-permute-done
  124.7 0.0 collective-permute-done.1
  124.7 3.9 broadcast_select_fusion.3
  128.6 1.2 collective-permute-start.2
  129.8 58.2 %shard_map.58 = (bf16[64,32,512]{2,1,0:T(8,128)(2,1)}, bf16[64,32,64,64]{3,2,1,0:T(8,128)(2,1)}, f32[32,64,512]{2,1,0:T(8,128)}, bf16[32,64,512]{2,1,0:T(8,128)(2,1)}, f32[32,64,512]{2,1,0:T(8,128)}) custom-call(s32[1]{0:T(128)} %bitcast.3.dead_ref, bf16[32,64,512]{2,1,0:T(8,128)(2,1)} %all-gather.5.cloned.1.call-done.own_ref, ...), custom_call_target="tpu_custom_call" | custom-call | flops 51539607552 | bytes 33554432 | tf_op jit(solution)/shard_map/pallas_call | solution.py:97
  188.0 2.2 collective-permute-start.3
  190.2 0.0 collective-permute-done.2.far_ref
  190.2 0.0 copy-start
  190.2 1.3 copy-done
  191.5 59.0 %shard_map.59 = (bf16[64,32,512]{2,1,0:T(8,128)(2,1)}, bf16[64,32,64,64]{3,2,1,0:T(8,128)(2,1)}, f32[32,64,512]{2,1,0:T(8,128)}, bf16[32,64,512]{2,1,0:T(8,128)(2,1)}, bf16[32,64,512]{2,1,0:T(8,128)(2,1)}) custom-call(s32[1]{0:T(128)} %bitcast.dead_ref, ...), custom_call_target="tpu_custom_call", output_to_operand_aliasing={{0}: (7, {}), {1}: (8, {})} | custom-call | flops 51539607552 | bytes 33554432 | tf_op jit(solution)/shard_map/pallas_call | solution.py:97
  250.5 4.5 %broadcast_select_fusion.1 = (bf16[32,64,512]{2,1,0:T(8,128)(2,1)}, bf16[32,64,512]{2,1,0:T(8,128)(2,1)}) fusion(bf16[32,64,512]{2,1,0:T(8,128)(2,1)} %get-tuple-element.28, bf16[32,64,512]{2,1,0:T(8,128)(2,1)} %get-tuple-element.29, pred[]{:T(512)S(6)} %eq.32, pred[]{:T(512)S(6)} %eq.33), kind=kLoop, calls=%fused_computation.12 | loop fusion | flops 2097152 | bytes 8388610 | tf_op jit(solution)/shard_map/jit(_where)/select_n | solution.py:133
  255.0 0.0 collective-permute-done.3
  255.0 0.0 collective-permute-start.4
  255.0 25.8 %collective-permute-done.4 = bf16[32,64,512]{2,1,0:T(8,128)(2,1)} collective-permute-done((bf16[32,64,512]{2,1,0:T(8,128)(2,1)}, bf16[32,64,512]{2,1,0:T(8,128)(2,1)}, u32[]{:S(2)}, u32[]{:S(2)}) %collective-permute-start.4) | collective-permute-done | bytes 2097184 | tf_op jit(solution)/shard_map/ppermute | solution.py:153
  280.8 5.1 %bitcast_bitcast_fusion.1 = bf16[4,32,64,128]{3,2,1,0:T(8,128)(2,1)} fusion(bf16[32,64,512]{2,1,0:T(8,128)(2,1)S(1)} %collective-permute-done.3, f32[32,64,512]{2,1,0:T(8,128)} %get-tuple-element.27, bf16[32,64,512]{2,1,0:T(8,128)(2,1)} %collective-permute-done.4, pred[]{:T(512)S(6)} %eq.34), kind=kLoop, calls=%fused_computation.9 | loop fusion | flops 6291456 | bytes 10485761 | tf_op jit(solution)/shard_map/transpose | solution.py:196
  285.9 0.0 reduce-scatter.3.cloned.1.call-update
  285.9 0.0 reduce-scatter.5.cloned.1.call-start
  286.0 2.3 collective-permute-start.5
  288.2 0.0 collective-permute-done.5
  288.2 4.4 bitcast_bitcast_fusion
  292.6 0.0 reduce-scatter.5.cloned.1.call-update
  292.6 88.1 %reduce-scatter.3.cloned.1.call-done = bf16[1,32,64,128]{3,2,1,0:T(8,128)(2,1)} async-done(((bf16[4,32,64,128]{3,2,1,0:T(8,128)(2,1)}), bf16[1,32,64,128]{3,2,1,0:T(8,128)(2,1)}) %reduce-scatter.3.cloned.1.call-update) | async-done | bytes 524304 | tf_op jit(solution)/shard_map/reduce_scatter | solution.py:197
  380.6 54.2 %reduce-scatter.5.cloned.1.call-done = bf16[1,32,64,128]{3,2,1,0:T(8,128)(2,1)} async-done(((bf16[4,32,64,128]{3,2,1,0:T(8,128)(2,1)}), bf16[1,32,64,128]{3,2,1,0:T(8,128)(2,1)}) %reduce-scatter.5.cloned.1.call-update) | async-done | bytes 524304 | tf_op jit(solution)/shard_map/reduce_scatter | solution.py:197
  434.9 2.7 convert_bitcast_fusion
Async XLA Ops:
  7.2 51.9 %all-gather.3.cloned.1.call-start = ((), (), s32[]{:S(2)}) async-start(), calls=%async_computation.2 | async-start | bytes 2621440 | tf_op jit(solution)/shard_map/all_gather | solution.py:156
  9.5 96.3 %all-gather.5.cloned.1.call-start = ((), (), s32[]{:S(2)}) async-start(), calls=%async_computation.3 | async-start | bytes 2621440 | tf_op jit(solution)/shard_map/all_gather | solution.py:156
  10.2 370.4 %reduce-scatter.3.cloned.1.call-start = ((), (), s32[]{:S(2)}) async-start(), calls=%async_computation.4 | async-start | bytes 2621440 | tf_op jit(solution)/shard_map/reduce_scatter | solution.py:197
  59.1 65.6 %collective-permute-start = (bf16[32,64,512]{2,1,0:T(8,128)(2,1)}, bf16[32,64,512]{2,1,0:T(8,128)(2,1)S(1)}, u32[]{:S(2)}, u32[]{:S(2)}) collective-permute-start(bf16[32,64,512]{2,1,0:T(8,128)(2,1)} %all-gather.3.cloned.1.call-done.own_ref), channel_id=1, source_target_pairs={{0,0},{1,1},{2,2},{3,3},{4,4},{5,5},{6,6},{7,7},{9,8},{10,9},{11,1... | collective-permute-start | bytes 6291464 | tf_op jit(solution)/shard_map/ppermute | solution.py:153
  105.7 19.0 %collective-permute-start.1 = (bf16[32,64,512]{2,1,0:T(8,128)(2,1)}, bf16[32,64,512]{2,1,0:T(8,128)(2,1)}, u32[]{:S(2)}, u32[]{:S(2)}) collective-permute-start(bf16[32,64,512]{2,1,0:T(8,128)(2,1)} %all-gather.5.cloned.1.call-done.own_ref), channel_id=1, source_target_pairs={{0,0},{1,1},{2,2},{3,3},{5,4},{6,5},{7,6},{4,7},{9,8},{10,9},{11,1... | collective-permute-start | bytes 6291464 | tf_op jit(solution)/shard_map/ppermute | solution.py:153
  128.6 61.6 %collective-permute-start.2 = (bf16[32,64,512]{2,1,0:T(8,128)(2,1)S(1)}, bf16[32,64,512]{2,1,0:T(8,128)(2,1)S(1)}, u32[]{:S(2)}, u32[]{:S(2)}) collective-permute-start(bf16[32,64,512]{2,1,0:T(8,128)(2,1)S(1)} %broadcast_select_fusion.4), channel_id=1, source_target_pairs={{1,0},{2,1},{3,2},{0,3},{5,4},{6,5},{7,6},{4,7},{10,8},{11,9},{8,1... | collective-permute-start | bytes 6291464 | tf_op jit(solution)/shard_map/ppermute | solution.py:153
  188.0 67.1 %collective-permute-start.3 = (bf16[32,64,512]{2,1,0:T(8,128)(2,1)}, bf16[32,64,512]{2,1,0:T(8,128)(2,1)S(1)}, u32[]{:S(2)}, u32[]{:S(2)}) collective-permute-start(bf16[32,64,512]{2,1,0:T(8,128)(2,1)} %get-tuple-element.30), channel_id=1, source_target_pairs={{0,0},{1,1},{2,2},{3,3},{4,4},{5,5},{6,6},{7,7},{8,9},{9,10},{10,1... | collective-permute-start | bytes 6291464 | tf_op jit(solution)/shard_map/ppermute | solution.py:153
  190.2 1.3 copy-start
  255.0 25.8 %collective-permute-start.4 = (bf16[32,64,512]{2,1,0:T(8,128)(2,1)}, bf16[32,64,512]{2,1,0:T(8,128)(2,1)}, u32[]{:S(2)}, u32[]{:S(2)}) collective-permute-start(bf16[32,64,512]{2,1,0:T(8,128)(2,1)} %get-tuple-element.31), channel_id=1, source_target_pairs={{0,1},{1,2},{2,3},{3,0},{4,5},{5,6},{6,7},{7,4},{8,10},{9,11},{10,... | collective-permute-start | bytes 6291464 | tf_op jit(solution)/shard_map/ppermute | solution.py:153
  285.9 149.0 %reduce-scatter.5.cloned.1.call-start = ((), (), s32[]{:S(2)}) async-start(), calls=%async_computation.5 | async-start | bytes 2621440 | tf_op jit(solution)/shard_map/reduce_scatter | solution.py:197
  286.0 2.3 collective-permute-start.5
Sparse Core Ops, SparseCore 0:
  10.1 48.9 all-gather.2
  61.2 44.4 all-gather.4
  286.0 94.5 reduce-scatter.2
  383.5 51.3 reduce-scatter.4

commit v3 on v2

--- a/solution.py
+++ b/solution.py
@@ -27,12 +27,12 @@
             pltpu.make_async_copy(far_ref, window.at[pl.ds(n_off, n_off)], sems.at[1]),
         ]
         if with_start:
-            copies.append(pltpu.make_async_copy(start_ref, col.at[pl.ds(0, n_off)], sems.at[2]))
+            copies.append(pltpu.make_async_copy(start_ref, col.at[pl.ds(n_off, n_off)], sems.at[2]))
         else:
-            col[0:n_off] = jnp.zeros((n_off, width, batch), F32)
+            col[n_off:] = jnp.zeros((n_off, width, batch), F32)
         for copy in copies:
             copy.start()
-        col[n_off:] = jnp.zeros((n_off, width, batch), F32)
+        col[0:n_off] = jnp.zeros((n_off, width, batch), F32)
         for copy in copies:
             copy.wait()
 
@@ -73,7 +73,7 @@
         col_far_ref[...] = col[n_off:].astype(col_far_ref.dtype)
 
 
-def pair_block(part, dead_from, own, up, weights, near, far, earlier, far_type):
+def pair_block(part, dead_from, own, up, weights, near, far, earlier, near_type):
     n_off, width = weights.shape[1], weights.shape[2]
     batch = own.shape[2]
     block = (n_off, width, batch)
@@ -109,8 +109,8 @@
             jax.ShapeDtypeStruct(up.shape, BF16),
             jax.ShapeDtypeStruct(weights.shape, BF16),
             jax.ShapeDtypeStruct(block, F32),
+            jax.ShapeDtypeStruct(block, near_type),
             jax.ShapeDtypeStruct(block, BF16),
-            jax.ShapeDtypeStruct(block, far_type),
         ],
         scratch_shapes=[
             pltpu.VMEM((2 * n_off, width, batch), BF16),
@@ -157,44 +157,47 @@
         for m in range(parts)
     ]
     fetched = [
-        moved(own[m], lambda r, m=m: (r + (m - r) % parts) // parts) for m in range(parts)
+        moved(own[m], lambda r, m=m: (r + (m - r - 1) % parts + 1) // parts)
+        for m in range(parts)
     ]
-    windows = [choose(fetched, (row_id + w) % parts) for w in range(parts)]
+    windows = [choose(fetched, (row_id + w) % parts) for w in range(1, parts + 1)]
     held = choose(own, row_id % parts)
-    held, windows[parts - 1] = lax.optimization_barrier((held, windows[parts - 1]))
-    windows.append(moved(held, lambda r: (r + parts) // parts))
-
-    row_parts, cols, earlier = [], [], []
-    for part in range(parts):
-        last = part == parts - 1
+    if parts > 1:
+        held, windows[-1] = lax.optimization_barrier((held, windows[-1]))
+    windows = [moved(held, lambda r: r // parts)] + windows
+
+    row_parts, cols, earlier = [None] * parts, [None] * (parts + 1), []
+    for part in reversed(range(parts)):
         dead_from = half_fields - col_id * a_dev - part * off_dev
         dead_from = jnp.where(row_id == n_rowf - 1, dead_from, off_dev).astype(jnp.int32)
-        interact, grad, row, near, far = pair_block(
+        interact, grad, row_parts[part], near, cols[part + 1] = pair_block(
             part, dead_from.reshape(1), own[part], up, pair_weights,
-            windows[part], windows[part + 1], earlier, BF16 if last else F32,
-        )
-        row_parts.append(row)
-        cols.append(near)
-        earlier = [far, interact, grad]
-    cols.append(far)
-    first_back = moved(cols[0], lambda r: r // parts, True)
-    outs = []
+            windows[part], windows[part + 1], earlier, BF16 if part == 0 else F32,
+        )
+        earlier = [near, interact, grad]
+    cols[0] = near
+    before = first_back = moved(cols[parts], lambda r: (r + parts) // parts, True)
     shape = (off_dev, emb.shape[1], n_rowf, emb.shape[2])
-    backs = []
-    for m in range(parts):
-        sent = choose(cols[1:], (m - row_id - 1) % parts)
-        if m == 0:
-            sent, first_back = lax.optimization_barrier((sent, first_back))
+    order = list(reversed(range(parts)))
+    backs = [None] * parts
+    for m in order:
+        sent = choose(cols[:parts], (m - row_id) % parts)
+        sent, before = lax.optimization_barrier((sent, before))
+        if m == order[0]:
+            first_back = before
         else:
-            sent, backs[-1] = lax.optimization_barrier((sent, backs[-1]))
-        backs.append(moved(sent, lambda r, m=m: (r + (m - r - 1) % parts + 1) // parts, True))
-    for m in range(parts):
-        if m > 0:
+            backs[m + 1] = before
+        before = moved(sent, lambda r, m=m: (r + (m - r) % parts) // parts, True)
+        backs[m] = before
+    outs = [None] * parts
+    summed = None
+    for m in order:
+        if summed is not None:
             backs[m], summed = lax.optimization_barrier((backs[m], summed))
         summed = row_parts[m] + backs[m].astype(F32)
         summed = summed + jnp.where(row_id % parts == m, first_back.astype(F32), 0.0)
         summed = jnp.transpose(summed.astype(BF16).reshape(shape), (2, 0, 1, 3))
-        outs.append(lax.psum_scatter(summed, "rowf", scatter_dimension=0, tiled=False))
+        outs[m] = lax.psum_scatter(summed, "rowf", scatter_dimension=0, tiled=False)
     grad_emb = jnp.concatenate(outs, axis=0).astype(F32)
     return (
         jnp.transpose(interact, (2, 0, 1)),

time: 446 us -> 419 us (0.939)
  waiting for transfers between devices: 262 us -> 240 us
    reduce_scatter x2, waiting for transfers between devices: 142 us -> 124 us  [shards(): outs[m] = lax.psum_scatter(summed, 'rowf', scatter_dimension=0, tiled=False)]
  transfers between devices with their start and end apart: 10 -> 10, of which waited for: 5 -> 5; matrix products, arithmetic and copies ran while one was open for 2% -> 3% of each run, Pallas kernels for 26% -> 28%
where the time goes in v3:
time: 419 us; the launch traced here: 418 us
  waiting for transfers between devices  240 us (57%)
  Pallas kernels  117 us (28%)
  starting transfers between devices  23 us (5%)
  other arithmetic  19.5 us (5%)
  between operations  13.8 us (3%)
    reduce_scatter x2, waiting for transfers between devices, shards(): outs[m] = lax.psum_scatter(summed, 'rowf', scatter_dimension=0, tiled=False)  124 us
    pallas_call x2, Pallas kernels, pair_block(): pl.pallas_call(functools.partial(pair_kernel, with_start=len(earlier) > 0...  117 us
    all_gather x2, waiting for transfers between devices, shards(): lax.all_gather(emb[m * off_dev:(m + 1) * off_dev], 'rowf', axis=2, tiled=...  93.2 us
    ppermute x6, starting transfers between devices, moved(): return lax.ppermute(block, ('rowf', 'colf'), pairs)  22.8 us
    ppermute x6, waiting for transfers between devices, moved(): return lax.ppermute(block, ('rowf', 'colf'), pairs)  22 us
    select_n x3, other arithmetic, choose(): out = jnp.where(index == at, options[at], out)  9.68 us
  transfers between devices with their start and end apart: 10, of which 5 were waited for; matrix products, arithmetic and copies ran while one was open for 3% of the time, Pallas kernels for 28%

profile of v3, /device:TPU:0, one launch (start us, length us, event | category | flops | bytes accessed | tf_op | source)
XLA Modules:
  0.0 417.5 jit_solution(16139627377634289821)
XLA Ops:
  7.2 0.0 all-gather.5.cloned.1.call-start
  7.2 2.2 fusion.6
  9.4 0.0 all-gather.5.cloned.1.call-update
  9.5 0.0 all-gather.3.cloned.1.call-start
  9.5 0.7 all-gather.3.cloned.1.call-update
  10.2 0.0 reduce-scatter.5.cloned.1.call-start
  10.3 48.8 %all-gather.5.cloned.1.call-done.own_ref = bf16[32,64,512]{2,1,0:T(8,128)(2,1)} async-done(((bf16[32,64,128]{2,1,0:T(8,128)(2,1)}), bf16[32,64,512]{2,1,0:T(8,128)(2,1)}) %all-gather.5.cloned.1.call-update) | async-done | bytes 2097168 | tf_op jit(solution)/shard_map/all_gather | solution.py:156
  59.1 2.2 collective-permute-start
  61.3 44.4 %all-gather.3.cloned.1.call-done.own_ref = bf16[32,64,512]{2,1,0:T(8,128)(2,1)} async-done(((bf16[32,64,128]{2,1,0:T(8,128)(2,1)}), bf16[32,64,512]{2,1,0:T(8,128)(2,1)}) %all-gather.3.cloned.1.call-update) | async-done | bytes 2097168 | tf_op jit(solution)/shard_map/all_gather | solution.py:156
  105.7 1.2 collective-permute-start.1
  106.9 1.8 broadcast_select_fusion.4
  108.8 0.0 collective-permute-done
  108.8 22.0 %collective-permute-done.1 = bf16[32,64,512]{2,1,0:T(8,128)(2,1)} collective-permute-done((bf16[32,64,512]{2,1,0:T(8,128)(2,1)}, bf16[32,64,512]{2,1,0:T(8,128)(2,1)}, u32[]{:S(2)}, u32[]{:S(2)}) %collective-permute-start.1) | collective-permute-done | bytes 2097184 | tf_op jit(solution)/shard_map/ppermute | solution.py:153
  130.8 3.9 broadcast_select_fusion.2
  134.7 0.8 collective-permute-start.2
  135.4 58.4 %shard_map.58 = (bf16[64,32,512]{2,1,0:T(8,128)(2,1)}, bf16[64,32,64,64]{3,2,1,0:T(8,128)(2,1)}, f32[32,64,512]{2,1,0:T(8,128)}, f32[32,64,512]{2,1,0:T(8,128)}, bf16[32,64,512]{2,1,0:T(8,128)(2,1)}) custom-call(s32[1]{0:T(128)} %bitcast.3.dead_ref, bf16[32,64,512]{2,1,0:T(8,128)(2,1)} %all-gather.5.cloned.1.call-done.own_ref, ...), custom_call_target="tpu_custom_call" | custom-call | flops 51539607552 | bytes 33554432 | tf_op jit(solution)/shard_map/pallas_call | solution.py:97
  193.9 0.7 collective-permute-start.3
  194.6 0.0 collective-permute-done.2.near_ref
  194.6 0.0 copy-start.1
  194.6 1.3 copy-done.1
  195.9 58.7 %shard_map.59 = (bf16[64,32,512]{2,1,0:T(8,128)(2,1)}, bf16[64,32,64,64]{3,2,1,0:T(8,128)(2,1)}, f32[32,64,512]{2,1,0:T(8,128)}, bf16[32,64,512]{2,1,0:T(8,128)(2,1)}, bf16[32,64,512]{2,1,0:T(8,128)(2,1)}) custom-call(s32[1]{0:T(128)} %bitcast.dead_ref, ...), custom_call_target="tpu_custom_call", output_to_operand_aliasing={{0}: (7, {}), {1}: (8, {})} | custom-call | flops 51539607552 | bytes 33554432 | tf_op jit(solution)/shard_map/pallas_call | solution.py:97
  254.6 0.0 copy-start
  254.6 4.0 broadcast_select_fusion.1
  258.6 0.0 collective-permute-done.3
  258.6 0.8 collective-permute-start.4
  259.4 0.0 collective-permute-done.4
  259.4 0.0 copy-done
  259.4 2.2 bitcast_bitcast_fusion.1
  261.6 0.0 reduce-scatter.5.cloned.1.call-update
  261.6 0.0 reduce-scatter.3.cloned.1.call-start
  261.7 17.1 %collective-permute-start.5 = (bf16[32,64,512]{2,1,0:T(8,128)(2,1)}, bf16[32,64,512]{2,1,0:T(8,128)(2,1)}, u32[]{:S(2)}, u32[]{:S(2)}) collective-permute-start(bf16[32,64,512]{2,1,0:T(8,128)(2,1)} %get-tuple-element.32), channel_id=1, source_target_pairs={{0,0},{1,1},{2,2},{3,3},{4,5},{5,6},{6,7},{7,4},{8,9},{9,10},{10,1... | collective-permute-start | bytes 6291464 | tf_op jit(solution)/shard_map/ppermute | solution.py:153
  278.8 0.0 collective-permute-done.5
  278.8 5.0 %bitcast_bitcast_fusion = bf16[4,32,64,128]{3,2,1,0:T(8,128)(2,1)} fusion(bf16[32,64,512]{2,1,0:T(8,128)(2,1)S(1)} %collective-permute-done.3, f32[32,64,512]{2,1,0:T(8,128)} %get-tuple-element.27, bf16[32,64,512]{2,1,0:T(8,128)(2,1)} %collective-permute-done.5, pred[]{:T(512)S(6)} %eq.37), kind=kLoop, calls=%fused_computation.8 | loop fusion | flops 6291456 | bytes 10485761 | tf_op jit(solution)/shard_map/transpose | solution.py:199
  283.8 0.0 reduce-scatter.3.cloned.1.call-update
  283.8 71.0 %reduce-scatter.5.cloned.1.call-done = bf16[1,32,64,128]{3,2,1,0:T(8,128)(2,1)} async-done(((bf16[4,32,64,128]{3,2,1,0:T(8,128)(2,1)}), bf16[1,32,64,128]{3,2,1,0:T(8,128)(2,1)}) %reduce-scatter.5.cloned.1.call-update) | async-done | bytes 524304 | tf_op jit(solution)/shard_map/reduce_scatter | solution.py:200
  354.8 53.5 %reduce-scatter.3.cloned.1.call-done = bf16[1,32,64,128]{3,2,1,0:T(8,128)(2,1)} async-done(((bf16[4,32,64,128]{3,2,1,0:T(8,128)(2,1)}), bf16[1,32,64,128]{3,2,1,0:T(8,128)(2,1)}) %reduce-scatter.3.cloned.1.call-update) | async-done | bytes 524304 | tf_op jit(solution)/shard_map/reduce_scatter | solution.py:200
  408.3 2.7 convert_bitcast_fusion
Async XLA Ops:
  7.2 51.9 %all-gather.5.cloned.1.call-start = ((), (), s32[]{:S(2)}) async-start(), calls=%async_computation.3 | async-start | bytes 2621440 | tf_op jit(solution)/shard_map/all_gather | solution.py:156
  9.5 96.3 %all-gather.3.cloned.1.call-start = ((), (), s32[]{:S(2)}) async-start(), calls=%async_computation.2 | async-start | bytes 2621440 | tf_op jit(solution)/shard_map/all_gather | solution.py:156
  10.2 344.6 %reduce-scatter.5.cloned.1.call-start = ((), (), s32[]{:S(2)}) async-start(), calls=%async_computation.5 | async-start | bytes 2621440 | tf_op jit(solution)/shard_map/reduce_scatter | solution.py:200
  59.1 49.7 %collective-permute-start = (bf16[32,64,512]{2,1,0:T(8,128)(2,1)}, bf16[32,64,512]{2,1,0:T(8,128)(2,1)S(1)}, u32[]{:S(2)}, u32[]{:S(2)}) collective-permute-start(bf16[32,64,512]{2,1,0:T(8,128)(2,1)} %all-gather.5.cloned.1.call-done.own_ref), channel_id=1, source_target_pairs={{0,0},{1,1},{2,2},{3,3},{5,4},{6,5},{7,6},{4,7},{9,8},{10,9},{11,1... | collective-permute-start | bytes 6291464 | tf_op jit(solution)/shard_map/ppermute | solution.py:153
  105.7 25.0 %collective-permute-start.1 = (bf16[32,64,512]{2,1,0:T(8,128)(2,1)}, bf16[32,64,512]{2,1,0:T(8,128)(2,1)}, u32[]{:S(2)}, u32[]{:S(2)}) collective-permute-start(bf16[32,64,512]{2,1,0:T(8,128)(2,1)} %all-gather.3.cloned.1.call-done.own_ref), channel_id=1, source_target_pairs={{1,0},{2,1},{3,2},{0,3},{5,4},{6,5},{7,6},{4,7},{10,8},{11,9},{8,1... | collective-permute-start | bytes 6291464 | tf_op jit(solution)/shard_map/ppermute | solution.py:153
  134.7 59.9 %collective-permute-start.2 = (bf16[32,64,512]{2,1,0:T(8,128)(2,1)S(1)}, bf16[32,64,512]{2,1,0:T(8,128)(2,1)S(1)}, u32[]{:S(2)}, u32[]{:S(2)}) collective-permute-start(bf16[32,64,512]{2,1,0:T(8,128)(2,1)S(1)} %broadcast_select_fusion.4), channel_id=1, source_target_pairs={{0,0},{1,1},{2,2},{3,3},{4,4},{5,5},{6,6},{7,7},{9,8},{10,9},{11,1... | collective-permute-start | bytes 6291464 | tf_op jit(solution)/shard_map/ppermute | solution.py:153
  193.9 64.7 %collective-permute-start.3 = (bf16[32,64,512]{2,1,0:T(8,128)(2,1)}, bf16[32,64,512]{2,1,0:T(8,128)(2,1)S(1)}, u32[]{:S(2)}, u32[]{:S(2)}) collective-permute-start(bf16[32,64,512]{2,1,0:T(8,128)(2,1)} %get-tuple-element.30), channel_id=1, source_target_pairs={{0,1},{1,2},{2,3},{3,0},{4,5},{5,6},{6,7},{7,4},{8,10},{9,11},{10,... | collective-permute-start | bytes 6291464 | tf_op jit(solution)/shard_map/ppermute | solution.py:153
  194.6 1.3 copy-start.1
  254.6 4.8 %copy-start = (f32[32,64,512]{2,1,0:T(8,128)S(1)}, f32[32,64,512]{2,1,0:T(8,128)}, u32[]{:S(2)}) copy-start(f32[32,64,512]{2,1,0:T(8,128)} %get-tuple-element.33) | copy-start | bytes 12582916
  258.6 0.8 collective-permute-start.4
  261.6 146.7 %reduce-scatter.3.cloned.1.call-start = ((), (), s32[]{:S(2)}) async-start(), calls=%async_computation.4 | async-start | bytes 2621440 | tf_op jit(solution)/shard_map/reduce_scatter | solution.py:200
  261.7 17.1 %collective-permute-start.5 = (bf16[32,64,512]{2,1,0:T(8,128)(2,1)}, bf16[32,64,512]{2,1,0:T(8,128)(2,1)}, u32[]{:S(2)}, u32[]{:S(2)}) collective-permute-start(bf16[32,64,512]{2,1,0:T(8,128)(2,1)} %get-tuple-element.32), channel_id=1, source_target_pairs={{0,0},{1,1},{2,2},{3,3},{4,5},{5,6},{6,7},{7,4},{8,9},{9,10},{10,1... | collective-permute-start | bytes 6291464 | tf_op jit(solution)/shard_map/ppermute | solution.py:153
Sparse Core Ops, SparseCore 0:
  10.1 48.9 all-gather.4
  61.2 44.4 all-gather.2
  261.8 93.0 reduce-scatter.4
  357.7 50.6 reduce-scatter.2
